TPU v7x, 128 devices: a whole 4x4x4 slice. The times are simulated.
128 devices in a mesh: rows: 16 (over y, z), feat: 8 (over x, core).
Axes of the slice: x: 4, y: 4, z: 4, core: 2. Of those that a mesh axis runs over, the one named last changes fastest.
Arguments:
- features: bfloat16 [32768, 1024], P('rows', 'feat'), may hold values from -6 to 6
- tiles: bfloat16 [10240, 128, 128], P('rows'), may hold values from -0.078125 to 0.078125
- tile_row: int32 [10240], P('rows'), may hold values from 0 to 15, as said below
- tile_panel: int32 [10240], P('rows'), may hold values from 0 to 15
- tile_slot: int32 [10240], P('rows'), may hold values from 0 to 7
- counts: int32 [16], P('rows'), may hold values from 1 to 640, as said below
- need_list: int32 [16, 16, 8], replicated, may hold values from 0 to 15, as said below
- weight: bfloat16 [1024, 1024], replicated, may hold values from -0.1875 to 0.1875
Outputs:
- activations: bfloat16 [32768, 1024], P(('rows', 'feat'))
Inputs may be any that keep to these rules, and one draw needn't show every extreme that they name: need_list[g, p] holds 8 distinct tile rows of panel p. Within a row group the slots name distinct (tile_row, tile_panel, tile_slot) triples. `counts`: some row group lists exactly 640 tiles.
All inputs are finite; a program needn't handle non-finite values.
Results may differ from a plain program's by a relative error of at most 0.0049.
Values may be sent and summed in bfloat16 or wider, within the bound.
A program may use at most 128 MiB of HBM per device.

v0:
```python
import math

import jax
import jax.numpy as jnp
from jax import lax
from jax.sharding import PartitionSpec as P

TILE = 128
TPP = 16
NEED = 8


def aggregate(source, block_ids, tiles, tile_row, live_slot, shard_width):
    slots = tiles.shape[0]
    per_step = math.gcd(slots, 128)
    steps_count = slots // per_step
    blocks = source.reshape(-1, TILE, shard_width)

    def one_step(total, inputs):
        tile_part, id_part, row_part, live_part = inputs
        fetched = jnp.take(blocks, id_part, axis=0)
        product = jnp.einsum("sij,sjh->sih", tile_part, fetched, preferred_element_type=jnp.float32)
        product = jnp.where(live_part[:, None, None], product, 0.0)
        return (total.at[row_part].add(product), None)

    initial = jnp.zeros((TPP, TILE, shard_width), jnp.float32)
    total, unused = lax.scan(
        one_step,
        initial,
        (
            tiles.reshape(steps_count, per_step, TILE, TILE),
            block_ids.reshape(steps_count, per_step),
            tile_row.reshape(steps_count, per_step),
            live_slot.reshape(steps_count, per_step),
        ),
    )
    return total.reshape(TPP * TILE, shard_width)


def per_device(features, tiles, tile_row, tile_panel, tile_slot, counts, need_list, weight):
    shard_width = features.shape[1]
    groups = lax.axis_size("rows")
    own_group = lax.axis_index("rows")
    live_slot = lax.broadcasted_iota(jnp.int32, tile_row.shape, 0) < counts[0]
    source = lax.all_gather(features, "rows", axis=0, tiled=True)
    own_table = lax.dynamic_index_in_dim(need_list, own_group, 0, keepdims=False).reshape(-1)
    flat_index = tile_panel * NEED + tile_slot
    matches = flat_index[:, None] == lax.broadcasted_iota(jnp.int32, (1, groups * NEED), 1)
    picked = jnp.sum(jnp.where(matches, own_table[None, :], 0), axis=1)
    block_ids = tile_panel * TPP + picked
    summed = aggregate(source, block_ids, tiles, tile_row, live_slot, shard_width)
    rounded = summed.astype(jnp.bfloat16)
    rows_full = lax.all_to_all(rounded, "feat", split_axis=0, concat_axis=1, tiled=True)
    mixed = jnp.dot(rows_full, weight, preferred_element_type=jnp.float32)
    return jnp.maximum(mixed, 0.0).astype(jnp.bfloat16)


def solution(mesh):
    return jax.shard_map(
        per_device,
        mesh=mesh,
        in_specs=(
            P("rows", "feat"),
            P("rows", None, None),
            P("rows"),
            P("rows"),
            P("rows"),
            P("rows"),
            P(),
            P(),
        ),
        out_specs=P(("rows", "feat"), None),
        check_vma=False,
    )
```

profile of v0, /device:TPU:1, one launch (start us, length us, event | category | flops | bytes accessed | tf_op | source)
XLA Modules:
  0.0 267.5 jit_solution(11468187125140343390)
XLA Ops:
  6.5 0.0 copy-start
  6.5 0.0 all-gather.2.cloned.1.call-start
  6.5 0.7 all-gather.2.cloned.1.call-update
  7.3 0.7 constant_dynamic-slice_fusion.2
  8.0 0.1 copy.13
  8.0 0.1 broadcast_in_dim.45
  8.8 0.7 multiply_add_fusion
  9.5 0.3 select_reduce_fusion
  9.8 0.7 add_bitcast_fusion
  10.5 73.1 %all-gather.2.cloned.1.call-done = bf16[32768,128]{1,0:T(8,128)(2,1)} async-done(((bf16[2048,128]{1,0:T(8,128)(2,1)}), bf16[32768,128]{1,0:T(8,128)(2,1)}) %all-gather.2.cloned.1.call-update) | async-done | bytes 8388624 | tf_op jit(solution)/shard_map/all_gather | solution.py:45
  83.6 0.1 broadcast_in_dim.44
  83.7 161.0 %while.10 = (s32[]{:T(128)}, f32[16,128,128]{2,1,0:T(8,128)S(1)}, s32[5,128]{1,0:T(8,128)}, pred[5,128]{1,0:T(8,128)(4,1)S(1)}, bf16[5,128,128,128]{3,2,1,0:T(8,...) while((s32[]{:T(128)}, f32[16,128,128]{2,1,0:T(8,128)S(1)}, ...), condition=%wide.region_3.4_spmd, body=%wide.region_1.3_spmd.sunk | while | flops 543164928 | bytes 50341088 | solution.py:27
  83.7 0.7 fusion.23
  84.4 6.4 %gather_fusion = bf16[128,128,128]{2,1,0:T(8,128)(2,1)} fusion(bf16[256,128,128]{2,1,0:T(8,128)(2,1)} %get-tuple-element.128, s32[1024]{0:T(1024)S(1)} %pad_clamp_fusion.2), kind=kCustom, calls=%fused_computation.clone.1 | custom fusion | bytes 8389120 | tf_op jit(solution)/shard_map/while/body/eval_jaxpr/jit(_take)/gather | solution.py:21
  90.9 8.0 %broadcast_select_fusion.2 = f32[128,128,128]{2,1,0:T(8,128)} fusion(pred[128]{0:T(512)(128)(4,1)S(1)} %dynamic-slice_bitcast_fusion.2, bf16[128,128,128]{2,1,0:T(8,128)(2,1)} %gather_fusion, pred[128]{0:T(512)(128)(4,1)S(1)} %compare_and_fusion.2, bf16[5,128,128,128]{3,2,1,0:T(8,128)(2,1)} %get-tuple-element.126, s32[]{:T(128)} %get-tuple-element.114), kind=kOutput, calls=%fused_computation.4.clone.1 | convolution fusion | flops 541065216 | bytes 16777984 | tf_op jit(solution)/shard_map/while/body/eval_jaxpr/sij,sjh->sih/dot_general | solution.py:22
  98.9 17.0 %scatter_fusion = f32[16,128,128]{2,1,0:T(8,128)S(1)} fusion(f32[16,128,128]{2,1,0:T(8,128)S(1)} %get-tuple-element.115, s32[128]{0:T(128)S(1)} %get-tuple-element.104, f32[128,128,128]{2,1,0:T(8,128)} %broadcast_select_fusion.2), kind=kCustom, calls=%fused_computation.1.clone.1 | custom fusion | flops 2097152 | bytes 25166336 | tf_op jit(solution)/shard_map/while/body/eval_jaxpr/scatter-add | solution.py:24
  115.9 0.7 fusion.23
  116.6 6.4 %gather_fusion = bf16[128,128,128]{2,1,0:T(8,128)(2,1)} fusion(bf16[256,128,128]{2,1,0:T(8,128)(2,1)} %get-tuple-element.128, s32[1024]{0:T(1024)S(1)} %pad_clamp_fusion.2), kind=kCustom, calls=%fused_computation.clone.1 | custom fusion | bytes 8389120 | tf_op jit(solution)/shard_map/while/body/eval_jaxpr/jit(_take)/gather | solution.py:21
  123.1 8.0 %broadcast_select_fusion.2 = f32[128,128,128]{2,1,0:T(8,128)} fusion(pred[128]{0:T(512)(128)(4,1)S(1)} %dynamic-slice_bitcast_fusion.2, bf16[128,128,128]{2,1,0:T(8,128)(2,1)} %gather_fusion, pred[128]{0:T(512)(128)(4,1)S(1)} %compare_and_fusion.2, bf16[5,128,128,128]{3,2,1,0:T(8,128)(2,1)} %get-tuple-element.126, s32[]{:T(128)} %get-tuple-element.114), kind=kOutput, calls=%fused_computation.4.clone.1 | convolution fusion | flops 541065216 | bytes 16777984 | tf_op jit(solution)/shard_map/while/body/eval_jaxpr/sij,sjh->sih/dot_general | solution.py:22
  131.1 17.0 %scatter_fusion = f32[16,128,128]{2,1,0:T(8,128)S(1)} fusion(f32[16,128,128]{2,1,0:T(8,128)S(1)} %get-tuple-element.115, s32[128]{0:T(128)S(1)} %get-tuple-element.104, f32[128,128,128]{2,1,0:T(8,128)} %broadcast_select_fusion.2), kind=kCustom, calls=%fused_computation.1.clone.1 | custom fusion | flops 2097152 | bytes 25166336 | tf_op jit(solution)/shard_map/while/body/eval_jaxpr/scatter-add | solution.py:24
  148.1 0.7 fusion.23
  148.8 6.4 %gather_fusion = bf16[128,128,128]{2,1,0:T(8,128)(2,1)} fusion(bf16[256,128,128]{2,1,0:T(8,128)(2,1)} %get-tuple-element.128, s32[1024]{0:T(1024)S(1)} %pad_clamp_fusion.2), kind=kCustom, calls=%fused_computation.clone.1 | custom fusion | bytes 8389120 | tf_op jit(solution)/shard_map/while/body/eval_jaxpr/jit(_take)/gather | solution.py:21
  155.3 8.0 %broadcast_select_fusion.2 = f32[128,128,128]{2,1,0:T(8,128)} fusion(pred[128]{0:T(512)(128)(4,1)S(1)} %dynamic-slice_bitcast_fusion.2, bf16[128,128,128]{2,1,0:T(8,128)(2,1)} %gather_fusion, pred[128]{0:T(512)(128)(4,1)S(1)} %compare_and_fusion.2, bf16[5,128,128,128]{3,2,1,0:T(8,128)(2,1)} %get-tuple-element.126, s32[]{:T(128)} %get-tuple-element.114), kind=kOutput, calls=%fused_computation.4.clone.1 | convolution fusion | flops 541065216 | bytes 16777984 | tf_op jit(solution)/shard_map/while/body/eval_jaxpr/sij,sjh->sih/dot_general | solution.py:22
  163.3 17.0 %scatter_fusion = f32[16,128,128]{2,1,0:T(8,128)S(1)} fusion(f32[16,128,128]{2,1,0:T(8,128)S(1)} %get-tuple-element.115, s32[128]{0:T(128)S(1)} %get-tuple-element.104, f32[128,128,128]{2,1,0:T(8,128)} %broadcast_select_fusion.2), kind=kCustom, calls=%fused_computation.1.clone.1 | custom fusion | flops 2097152 | bytes 25166336 | tf_op jit(solution)/shard_map/while/body/eval_jaxpr/scatter-add | solution.py:24
  180.4 0.7 fusion.23
  181.1 6.4 %gather_fusion = bf16[128,128,128]{2,1,0:T(8,128)(2,1)} fusion(bf16[256,128,128]{2,1,0:T(8,128)(2,1)} %get-tuple-element.128, s32[1024]{0:T(1024)S(1)} %pad_clamp_fusion.2), kind=kCustom, calls=%fused_computation.clone.1 | custom fusion | bytes 8389120 | tf_op jit(solution)/shard_map/while/body/eval_jaxpr/jit(_take)/gather | solution.py:21
  187.5 8.0 %broadcast_select_fusion.2 = f32[128,128,128]{2,1,0:T(8,128)} fusion(pred[128]{0:T(512)(128)(4,1)S(1)} %dynamic-slice_bitcast_fusion.2, bf16[128,128,128]{2,1,0:T(8,128)(2,1)} %gather_fusion, pred[128]{0:T(512)(128)(4,1)S(1)} %compare_and_fusion.2, bf16[5,128,128,128]{3,2,1,0:T(8,128)(2,1)} %get-tuple-element.126, s32[]{:T(128)} %get-tuple-element.114), kind=kOutput, calls=%fused_computation.4.clone.1 | convolution fusion | flops 541065216 | bytes 16777984 | tf_op jit(solution)/shard_map/while/body/eval_jaxpr/sij,sjh->sih/dot_general | solution.py:22
  195.5 17.0 %scatter_fusion = f32[16,128,128]{2,1,0:T(8,128)S(1)} fusion(f32[16,128,128]{2,1,0:T(8,128)S(1)} %get-tuple-element.115, s32[128]{0:T(128)S(1)} %get-tuple-element.104, f32[128,128,128]{2,1,0:T(8,128)} %broadcast_select_fusion.2), kind=kCustom, calls=%fused_computation.1.clone.1 | custom fusion | flops 2097152 | bytes 25166336 | tf_op jit(solution)/shard_map/while/body/eval_jaxpr/scatter-add | solution.py:24
  212.6 0.7 fusion.23
  213.3 6.4 %gather_fusion = bf16[128,128,128]{2,1,0:T(8,128)(2,1)} fusion(bf16[256,128,128]{2,1,0:T(8,128)(2,1)} %get-tuple-element.128, s32[1024]{0:T(1024)S(1)} %pad_clamp_fusion.2), kind=kCustom, calls=%fused_computation.clone.1 | custom fusion | bytes 8389120 | tf_op jit(solution)/shard_map/while/body/eval_jaxpr/jit(_take)/gather | solution.py:21
  219.7 8.0 %broadcast_select_fusion.2 = f32[128,128,128]{2,1,0:T(8,128)} fusion(pred[128]{0:T(512)(128)(4,1)S(1)} %dynamic-slice_bitcast_fusion.2, bf16[128,128,128]{2,1,0:T(8,128)(2,1)} %gather_fusion, pred[128]{0:T(512)(128)(4,1)S(1)} %compare_and_fusion.2, bf16[5,128,128,128]{3,2,1,0:T(8,128)(2,1)} %get-tuple-element.126, s32[]{:T(128)} %get-tuple-element.114), kind=kOutput, calls=%fused_computation.4.clone.1 | convolution fusion | flops 541065216 | bytes 16777984 | tf_op jit(solution)/shard_map/while/body/eval_jaxpr/sij,sjh->sih/dot_general | solution.py:22
  227.7 17.0 %scatter_fusion = f32[16,128,128]{2,1,0:T(8,128)S(1)} fusion(f32[16,128,128]{2,1,0:T(8,128)S(1)} %get-tuple-element.115, s32[128]{0:T(128)S(1)} %get-tuple-element.104, f32[128,128,128]{2,1,0:T(8,128)} %broadcast_select_fusion.2), kind=kCustom, calls=%fused_computation.1.clone.1 | custom fusion | flops 2097152 | bytes 25166336 | tf_op jit(solution)/shard_map/while/body/eval_jaxpr/scatter-add | solution.py:24
  244.8 0.1 convert_element_type.10
  244.9 14.1 %all_to_all.16 = bf16[8,256,128]{2,1,0:T(8,128)(2,1)S(1)} all-to-all(bf16[8,256,128]{2,1,0:T(8,128)(2,1)S(1)} %bitcast.45), channel_id=1, replica_groups=mesh['rows'=16,'feat'=8] {'feat'}, dimensions={0} | all-to-all | bytes 1048576 | tf_op jit(solution)/shard_map/all_to_all | solution.py:53
  258.9 0.2 copy.14
  259.2 0.0 copy-done
  259.2 1.5 fusion.15
  (16 shorter events, 0.2 us)
Async XLA Ops:
  6.5 252.6 %copy-start = (bf16[1024,1024]{1,0:T(8,128)(2,1)S(1)}, bf16[1024,1024]{1,0:T(8,128)(2,1)}, u32[]{:S(2)}) copy-start(bf16[1024,1024]{1,0:T(8,128)(2,1)} %param.17) | copy-start | bytes 6291460
  6.5 77.1 %all-gather.2.cloned.1.call-start = ((), (), s32[]{:S(2)}) async-start(), calls=%async_computation.1 | async-start | bytes 8912896 | tf_op jit(solution)/shard_map/all_gather | solution.py:45
Sparse Core Ops, SparseCore 0:
  9.5 74.0 all-gather.1
where the time goes:
time: 270 us; the launch traced here: 268 us
  other arithmetic  90.5 us (34%)
  waiting for transfers between devices  73.9 us (27%)
  matrix products  41.6 us (15%)
  local copies, waits for them, and re-layouts  33.2 us (12%)
  blocking collectives  14.1 us (5%)
  between operations  14.1 us (5%)
    scatter-add x5, other arithmetic, one_step(): return (total.at[row_part].add(product), None)  85.2 us
    all_gather x1, waiting for transfers between devices, per_device(): source = lax.all_gather(features, 'rows', axis=0, tiled=True)  73.1 us
    dot_general x5, matrix products, one_step(): jnp.einsum('sij,sjh->sih', tile_part, fetched, preferred_element_type=jnp...  40.1 us
    gather x5, local copies, waits for them, and re-layouts, one_step(): fetched = jnp.take(blocks, id_part, axis=0)  32 us
    all_to_all x1, blocking collectives, per_device(): lax.all_to_all(rounded, 'feat', split_axis=0, concat_axis=1, tiled=True)  14.1 us
  transfers between devices with their start and end apart: 1, of which 1 were waited for; matrix products, arithmetic and copies ran while one was open for 1% of the time, Pallas kernels for 0%

commit v1 on v0

v1 whole, which is shorter than its diff:
```python
import functools

import jax
import jax.numpy as jnp
from jax import lax
from jax.experimental import pallas as pl
from jax.experimental.pallas import tpu as pltpu
from jax.sharding import PartitionSpec as P

TILE = 128
TPP = 16
NEED = 8
GROUPS = 16
FEAT = 8
MAXT = 640
CHUNKS = 4
PER = TPP // CHUNKS
TILE_DMAS = 8
MESH = pl.DeviceIdType.MESH

INNER = {4: (0, 2), 8: (0, 3), 6: (4, 1), 9: (8, 0), 11: (9, 1)}
LEAF = {1: (0, 0), 2: (0, 1), 10: (8, 1), 12: (8, 2), 5: (4, 0), 13: (9, 2), 7: (6, 0), 14: (6, 3), 3: (11, 3), 15: (11, 2)}
INNER_LIST = [4, 8, 6, 9, 11]
LEAF_LIST = list(LEAF)
HELD = [0] + INNER_LIST
ORDER = [0, 8, 4, 9, 6, 1, 12, 11, 2, 10, 5, 13, 7, 14, 3, 15]
CHILD = {4: [6], 8: [9], 9: [11]}

BEFORE = [
    ("in", 8, 0), ("in", 4, 0), ("in", 8, 1), ("in", 4, 1), ("in", 8, 2), ("in", 9, 0), ("in", 8, 3), ("in", 4, 2),
]
STEPS = {
    0: [("use", 0)],
    1: [("use", 8), ("in", 9, 1)],
    2: [("in", 4, 3), ("in", 9, 2), ("use", 4), ("send", 1), ("send", 12)],
    3: [("in", 9, 3), ("use", 9), ("send", 5), ("send", 13)],
    4: [("in", 6, 0), ("in", 6, 1), ("in", 6, 2), ("in", 6, 3), ("use", 6), ("send", 2), ("send", 10), ("send", 7), ("send", 14)],
    5: [("get", 1)],
    6: [("get", 12)],
    7: [("in", 11, 0), ("in", 11, 1), ("in", 11, 2), ("in", 11, 3), ("use", 11), ("send", 3), ("send", 15)],
    8: [("get", 2)],
    9: [("get", 10)],
    10: [("get", 5)],
    11: [("get", 13)],
    12: [("get", 7)],
    13: [("get", 14)],
    14: [("get", 3)],
    15: [("get", 15)],
}


def flip(c, bits):
    return (c, c + 1 - 2 * (c % 2), 3 - c, (c + 2) % 4)[bits]


def layer_kernel(features, tiles, row_hbm, panel_hbm, slot_hbm, count_hbm, need_hbm, weight, out,
                 held0, held1, held2, held3, held4, held5, parts, outbox, tile_mem, table_vec, table, row_mem, panel_mem,
                 slot_mem, count_mem, need_mem, panel_of, total, weight_mem, mail, inbox,
                 local_sem, tile_sem, small_sem, inner_send, inner_recv, leaf_send, leaf_recv, mail_send, mail_recv):
    group, member = lax.axis_index("rows"), lax.axis_index("feat")
    core = member % 2
    y, z = group // 4, group % 4
    first, second = y + core * (z - y), z + core * (y - z)
    held = dict(zip(HELD, (held0, held1, held2, held3, held4, held5)))

    def group_at(v):
        a, b = flip(first, v & 3), flip(second, v >> 2)
        return (a + core * (b - a)) * 4 + b + core * (a - b)

    own_copy = pltpu.make_async_copy(features, held0, local_sem.at[0])
    own_copy.start()
    small = [
        pltpu.make_async_copy(row_hbm, row_mem, small_sem.at[0]),
        pltpu.make_async_copy(panel_hbm, panel_mem, small_sem.at[1]),
        pltpu.make_async_copy(slot_hbm, slot_mem, small_sem.at[2]),
        pltpu.make_async_copy(count_hbm, count_mem, small_sem.at[3]),
        pltpu.make_async_copy(need_hbm.at[group], need_mem.at[0], small_sem.at[4]),
    ] + [
        pltpu.make_async_copy(need_hbm.at[group_at(1 << d)], need_mem.at[1 + d], small_sem.at[5 + d]) for d in range(4)
    ]
    for copy in small:
        copy.start()

    barrier = pltpu.get_barrier_semaphore()
    for d in range(4):
        pl.semaphore_signal(barrier, inc=1, device_id=(group_at(1 << d), member), device_id_type=MESH)
    for step in range(1, FEAT):
        pl.semaphore_signal(barrier, inc=1, device_id=(group, (member + step) % FEAT), device_id_type=MESH)

    share = MAXT // TILE_DMAS
    tile_copies = [
        pltpu.make_async_copy(tiles.at[pl.ds(i * share, share)], tile_mem.at[pl.ds(i * share, share)], tile_sem.at[i])
        for i in range(TILE_DMAS)
    ]
    weight_copy = pltpu.make_async_copy(weight, weight_mem, local_sem.at[1])

    def inner_copy(w, c):
        v, d = INNER[w]
        i = INNER_LIST.index(w) * CHUNKS + c
        rows = pl.ds(c * PER, PER)
        return pltpu.make_async_remote_copy(
            src_ref=held[v].at[rows], dst_ref=held[w].at[rows], send_sem=inner_send.at[i], recv_sem=inner_recv.at[i],
            device_id=(group_at(1 << d), member), device_id_type=MESH)

    def leaf_copy(w):
        d = LEAF[w][1]
        i = LEAF_LIST.index(w)
        return pltpu.make_async_remote_copy(
            src_ref=outbox.at[i], dst_ref=parts.at[ORDER.index(w)], send_sem=leaf_send.at[i], recv_sem=leaf_recv.at[i],
            device_id=(group_at(1 << d), member), device_id_type=MESH)

    def perform(event):
        kind, v = event[0], event[1]
        if kind == "in":
            inner_copy(v, event[2]).wait_recv()
            for w in CHILD.get(v, []):
                inner_copy(w, event[2]).start()
        elif kind == "use":
            k, panel = ORDER.index(v), group_at(v)
            for s in range(NEED):
                parts[k, s] = held[v][need_mem[0, panel, s]]
        elif kind == "send":
            u, d = LEAF[v]
            i, panel = LEAF_LIST.index(v), group_at(u)
            for s in range(NEED):
                outbox[i, s] = held[u][need_mem[1 + d, panel, s]]
            leaf_copy(v).start()
        else:
            leaf_copy(v).wait_recv()

    own_copy.wait()
    pl.semaphore_wait(barrier, 4 + FEAT - 1)
    for c in range(CHUNKS):
        inner_copy(8, c).start()
        inner_copy(4, c).start()
    for copy in tile_copies:
        copy.start()
    weight_copy.start()
    for copy in small:
        copy.wait()

    for k, v in enumerate(ORDER):
        panel_of[k] = group_at(v)
    count = count_mem[0]
    place = lax.broadcasted_iota(jnp.int32, (TPP, TILE), 0) * TILE + lax.broadcasted_iota(jnp.int32, (TPP, TILE), 1)

    def enter(k, found):
        code = row_mem[k] * TILE + panel_mem[k] * NEED + slot_mem[k]
        code = jnp.where(k < count, code, -1)
        return jnp.where(place == code, k, found)

    table_vec[...] = lax.fori_loop(0, MAXT, enter, jnp.full((TPP, TILE), MAXT, jnp.int32), unroll=8)
    table_copy = pltpu.make_async_copy(table_vec, table, local_sem.at[2])
    table_copy.start()
    tile_mem[MAXT] = jnp.zeros((TILE, TILE), jnp.bfloat16)
    total[...] = jnp.zeros_like(total)
    table_copy.wait()

    for event in BEFORE:
        perform(event)
    for copy in tile_copies:
        copy.wait()

    def step(k, carry):
        for at, events in STEPS.items():
            @pl.when(k == at)
            def _():
                for event in events:
                    perform(event)
        column = panel_of[k] * NEED
        block = parts[k].reshape(NEED * TILE, TILE)
        for r in range(TPP):
            row = jnp.concatenate([tile_mem[table[r, column + s]] for s in range(NEED)], axis=1)
            total[r * TILE:(r + 1) * TILE, :] += jnp.dot(row, block, preferred_element_type=jnp.float32)
        return carry

    lax.fori_loop(0, TPP, step, 0)

    share_rows = TPP * TILE // FEAT
    order = [4, 5, 3, 2, 6, 7, 1]

    def mail_copy(step):
        to = (member + step) % FEAT
        return pltpu.make_async_remote_copy(
            src_ref=mail.at[to], dst_ref=inbox.at[member], send_sem=mail_send.at[step - 1], recv_sem=mail_recv.at[step - 1],
            device_id=(group, to), device_id_type=MESH)

    for n in order:
        to = (member + n) % FEAT
        mail[to] = total[pl.ds(pl.multiple_of(to * share_rows, share_rows), share_rows), :].astype(jnp.bfloat16)
        mail_copy(n).start()
    inbox[member] = total[pl.ds(pl.multiple_of(member * share_rows, share_rows), share_rows), :].astype(jnp.bfloat16)
    weight_copy.wait()
    for n in order:
        mail_copy(n).wait_recv()
    rows = jnp.concatenate([inbox[j] for j in range(FEAT)], axis=1)
    width = 256
    for c in range(out.shape[1] // width):
        cols = slice(c * width, (c + 1) * width)
        mixed = jnp.dot(rows, weight_mem[:, cols], preferred_element_type=jnp.float32)
        out[:, cols] = jnp.maximum(mixed, 0.0).astype(out.dtype)
    for w in INNER_LIST:
        for c in range(CHUNKS):
            inner_copy(w, c).wait_send()
    for w in LEAF_LIST:
        leaf_copy(w).wait_send()
    for n in order:
        mail_copy(n).wait_send()


def per_device(features, tiles, tile_row, tile_panel, tile_slot, counts, need_list, weight):
    width = features.shape[1]
    hidden = weight.shape[1]
    share_rows = TPP * TILE // FEAT
    any_spec = pl.BlockSpec(memory_space=pl.ANY)
    bf16 = jnp.bfloat16
    dma = pltpu.SemaphoreType.DMA
    return pl.pallas_call(
        layer_kernel,
        out_shape=jax.ShapeDtypeStruct((share_rows, hidden), bf16),
        in_specs=[any_spec] * 8,
        out_specs=pl.BlockSpec(memory_space=pltpu.VMEM),
        scratch_shapes=[pltpu.VMEM((TPP, TILE, width), bf16)] * 6 + [
            pltpu.VMEM((GROUPS, NEED, TILE, width), bf16),
            pltpu.VMEM((len(LEAF), NEED, TILE, width), bf16),
            pltpu.VMEM((MAXT + 1, TILE, TILE), bf16),
            pltpu.VMEM((TPP, TILE), jnp.int32),
            pltpu.SMEM((TPP, TILE), jnp.int32),
            pltpu.SMEM((MAXT,), jnp.int32),
            pltpu.SMEM((MAXT,), jnp.int32),
            pltpu.SMEM((MAXT,), jnp.int32),
            pltpu.SMEM((1,), jnp.int32),
            pltpu.SMEM((5, GROUPS, NEED), jnp.int32),
            pltpu.SMEM((GROUPS,), jnp.int32),
            pltpu.VMEM((TPP * TILE, width), jnp.float32),
            pltpu.VMEM((FEAT * width, hidden), bf16),
            pltpu.VMEM((FEAT, share_rows, width), bf16),
            pltpu.VMEM((FEAT, share_rows, width), bf16),
            dma((3,)), dma((TILE_DMAS,)), dma((9,)),
            dma((len(INNER) * CHUNKS,)), dma((len(INNER) * CHUNKS,)),
            dma((len(LEAF),)), dma((len(LEAF),)),
            dma((FEAT - 1,)), dma((FEAT - 1,)),
        ],
        compiler_params=pltpu.CompilerParams(collective_id=0, has_side_effects=True, vmem_limit_bytes=56 * 2**20),
        cost_estimate=pl.CostEstimate(flops=9 * 10**9, bytes_accessed=25 * 10**6, transcendentals=0),
    )(features.reshape(TPP, TILE, width), tiles, tile_row, tile_panel, tile_slot, counts, need_list, weight)


def solution(mesh):
    return jax.shard_map(
        per_device,
        mesh=mesh,
        in_specs=(P("rows", "feat"), P("rows", None, None), P("rows"), P("rows"), P("rows"), P("rows"), P(), P()),
        out_specs=P(("rows", "feat"), None),
        check_vma=False,
    )
```

time: 270 us -> 61.8 us (0.23)
  other arithmetic: 90.5 us -> 0 us
  waiting for transfers between devices: 73.9 us -> 0 us
  Pallas kernels: 0 us -> 57.5 us
  matrix products: 41.6 us -> 0 us
  local copies, waits for them, and re-layouts: 33.2 us -> 3.46 us
  blocking collectives: 14.1 us -> 0 us
  between operations: 14.1 us -> 0.66 us
    scatter-add x5 -> x0, other arithmetic: 85.2 us -> none  [one_step(): return (total.at[row_part].add(product), None)]
    all_gather x1 -> x0, waiting for transfers between devices: 73.1 us -> none  [per_device(): source = lax.all_gather(features, 'rows', axis=0, tiled=True)]
    pallas_call x0 -> x1, Pallas kernels: none -> 57.5 us  [per_device(): pl.pallas_call(layer_kernel, out_shape=jax.ShapeDtypeStruct((share_rows,...]
    dot_general x6 -> x0, matrix products: 41.6 us -> none  [the longest x5 40.1 us: one_step(): jnp.einsum('sij,sjh->sih', tile_part, fetched, preferred_element_type=jnp...]
    gather x5 -> x0, local copies, waits for them, and re-layouts: 32 us -> none  [one_step(): fetched = jnp.take(blocks, id_part, axis=0)]
    all_to_all x1 -> x0, blocking collectives: 14.1 us -> none  [per_device(): lax.all_to_all(rounded, 'feat', split_axis=0, concat_axis=1, tiled=True)]
    select_n x5 -> x0, other arithmetic: 3.49 us -> none  [one_step(): fetched = jnp.take(blocks, id_part, axis=0)]
    unnamed x2, local copies, waits for them, and re-layouts: 0.01 us -> 3.46 us
  transfers between devices with their start and end apart: 1 -> 0, of which waited for: 1 -> 0; matrix products, arithmetic and copies ran while one was open for 1% -> 0% of each run, Pallas kernels for 0% -> 0%
where the time goes in v1:
time: 61.8 us; the launch traced here: 61.6 us
  Pallas kernels  57.5 us (93%)
  local copies, waits for them, and re-layouts  3.46 us (6%)
  between operations  0.66 us (1%)
    pallas_call x1, Pallas kernels, per_device(): pl.pallas_call(layer_kernel, out_shape=jax.ShapeDtypeStruct((share_rows,...  57.5 us
    unnamed x2, local copies, waits for them, and re-layouts  3.46 us

profile of v1, /device:TPU:1, one launch (start us, length us, event | category | flops | bytes accessed | tf_op | source)
XLA Modules:
  0.0 61.6 jit_solution(8587990729367440865)
XLA Ops:
  0.7 1.6 %copy.9.need_hbm = s32[16,16,8]{2,1,0:T(8,128)} copy(s32[16,16,8]{1,2,0:T(8,128)} %param.14) | data formatting | bytes 16384 | tf_op args[6]
  2.2 57.5 %shard_map.82 = bf16[256,1024]{1,0:T(8,128)(2,1)} custom-call(bf16[16,128,128]{2,1,0:T(8,128)(2,1)} %bitcast.1, bf16[640,128,128]{2,1,0:T(8,128)(2,1)} %tiles.1, s32[640]{0:T(1024)} %row_hbm.1, s32[640]{0:T(1024)} %panel_hbm.1, s32[640]{0:T(1024)} %slot_hbm.1, s32[1]{0:T(128)S(6)} %copy.11.count_hbm, s32[16,16,8]{2,1,0:T(8,128)} %copy.9.need_hbm, ...), custom_call_target="tpu_custom_call" | custom-call | flops 8999999488 | bytes 25000000 | tf_op jit(solution)/shard_map/pallas_call | solution.py:218
  59.7 1.9 %copy.12 = bf16[256,1024]{1,0:T(8,128)(2,1)} copy(bf16[256,1024]{1,0:T(8,128)(2,1)} %shard_map.82) | data formatting | bytes 1048576

commit v2 on v1

--- a/solution.py
+++ b/solution.py
@@ -23,8 +23,12 @@
 INNER_LIST = [4, 8, 6, 9, 11]
 LEAF_LIST = list(LEAF)
 HELD = [0] + INNER_LIST
-ORDER = [0, 8, 4, 9, 6, 1, 12, 11, 2, 10, 5, 13, 7, 14, 3, 15]
+ORDER = [0, 8, 4, 9, 6, 1, 12, 11, 2, 14, 5, 13, 7, 15, 3, 10]
 CHILD = {4: [6], 8: [9], 9: [11]}
+
+HALF = NEED // 2
+SPLIT = 4
+N_FULL = len(ORDER) - SPLIT
 
 BEFORE = [
     ("in", 8, 0), ("in", 4, 0), ("in", 8, 1), ("in", 4, 1), ("in", 8, 2), ("in", 9, 0), ("in", 8, 3), ("in", 4, 2),
@@ -33,19 +37,15 @@
     0: [("use", 0)],
     1: [("use", 8), ("in", 9, 1)],
     2: [("in", 4, 3), ("in", 9, 2), ("use", 4), ("send", 1), ("send", 12)],
-    3: [("in", 9, 3), ("use", 9), ("send", 5), ("send", 13)],
-    4: [("in", 6, 0), ("in", 6, 1), ("in", 6, 2), ("in", 6, 3), ("use", 6), ("send", 2), ("send", 10), ("send", 7), ("send", 14)],
+    3: [("in", 9, 3), ("use", 9)],
+    4: [("in", 6, 0), ("in", 6, 1), ("in", 6, 2), ("in", 6, 3), ("use", 6), ("send", 2), ("send", 14), ("send", 5), ("send", 13)],
     5: [("get", 1)],
     6: [("get", 12)],
-    7: [("in", 11, 0), ("in", 11, 1), ("in", 11, 2), ("in", 11, 3), ("use", 11), ("send", 3), ("send", 15)],
+    7: [("in", 11, 0), ("in", 11, 1), ("in", 11, 2), ("in", 11, 3), ("use", 11), ("send", 7), ("send", 15), ("send", 3), ("send", 10)],
     8: [("get", 2)],
-    9: [("get", 10)],
+    9: [("get", 14)],
     10: [("get", 5)],
     11: [("get", 13)],
-    12: [("get", 7)],
-    13: [("get", 14)],
-    14: [("get", 3)],
-    15: [("get", 15)],
 }
 
 
@@ -55,7 +55,7 @@
 
 def layer_kernel(features, tiles, row_hbm, panel_hbm, slot_hbm, count_hbm, need_hbm, weight, out,
                  held0, held1, held2, held3, held4, held5, parts, outbox, tile_mem, table_vec, table, row_mem, panel_mem,
-                 slot_mem, count_mem, need_mem, panel_of, total, weight_mem, mail, inbox,
+                 slot_mem, count_mem, need_mem, panel_of, total, weight_mem, mail, inbox, mixed,
                  local_sem, tile_sem, small_sem, inner_send, inner_recv, leaf_send, leaf_recv, mail_send, mail_recv):
     group, member = lax.axis_index("rows"), lax.axis_index("feat")
     core = member % 2
@@ -93,6 +93,8 @@
         for i in range(TILE_DMAS)
     ]
     weight_copy = pltpu.make_async_copy(weight, weight_mem, local_sem.at[1])
+    for copy in tile_copies + [weight_copy]:
+        copy.start()
 
     def inner_copy(w, c):
         v, d = INNER[w]
@@ -102,11 +104,13 @@
             src_ref=held[v].at[rows], dst_ref=held[w].at[rows], send_sem=inner_send.at[i], recv_sem=inner_recv.at[i],
             device_id=(group_at(1 << d), member), device_id_type=MESH)
 
-    def leaf_copy(w):
+    def leaf_copy(w, part):
         d = LEAF[w][1]
         i = LEAF_LIST.index(w)
+        blocks = pl.ds(part * HALF, HALF)
         return pltpu.make_async_remote_copy(
-            src_ref=outbox.at[i], dst_ref=parts.at[ORDER.index(w)], send_sem=leaf_send.at[i], recv_sem=leaf_recv.at[i],
+            src_ref=outbox.at[i, blocks], dst_ref=parts.at[ORDER.index(w), blocks], send_sem=leaf_send.at[2 * i + part],
+            recv_sem=leaf_recv.at[2 * i + part],
             device_id=(group_at(1 << d), member), device_id_type=MESH)
 
     def perform(event):
@@ -118,24 +122,23 @@
         elif kind == "use":
             k, panel = ORDER.index(v), group_at(v)
             for s in range(NEED):
-                parts[k, s] = held[v][need_mem[0, panel, s]]
+                parts[k, s] = held[v][need_mem[0, s, panel]]
         elif kind == "send":
             u, d = LEAF[v]
             i, panel = LEAF_LIST.index(v), group_at(u)
             for s in range(NEED):
-                outbox[i, s] = held[u][need_mem[1 + d, panel, s]]
-            leaf_copy(v).start()
+                outbox[i, s] = held[u][need_mem[1 + d, s, panel]]
+            for part in range(2):
+                leaf_copy(v, part).start()
         else:
-            leaf_copy(v).wait_recv()
+            for part in range(2):
+                leaf_copy(v, part).wait_recv()
 
     own_copy.wait()
     pl.semaphore_wait(barrier, 4 + FEAT - 1)
     for c in range(CHUNKS):
         inner_copy(8, c).start()
         inner_copy(4, c).start()
-    for copy in tile_copies:
-        copy.start()
-    weight_copy.start()
     for copy in small:
         copy.wait()
 
@@ -174,38 +177,82 @@
             total[r * TILE:(r + 1) * TILE, :] += jnp.dot(row, block, preferred_element_type=jnp.float32)
         return carry
 
-    lax.fori_loop(0, TPP, step, 0)
-
+    lax.fori_loop(0, N_FULL, step, 0)
+
+    def early(t, carry):
+        for at in range(SPLIT):
+            @pl.when(t == at)
+            def _():
+                leaf_copy(ORDER[N_FULL + at], 0).wait_recv()
+        k = N_FULL + t
+        column = panel_of[k] * NEED
+        block = parts[k, :HALF].reshape(HALF * TILE, TILE)
+        for r in range(TPP):
+            row = jnp.concatenate([tile_mem[table[r, column + s]] for s in range(HALF)], axis=1)
+            total[r * TILE:(r + 1) * TILE, :] += jnp.dot(row, block, preferred_element_type=jnp.float32)
+        return carry
+
+    lax.fori_loop(0, SPLIT, early, 0)
+
+    for v in ORDER[N_FULL:]:
+        leaf_copy(v, 1).wait_recv()
     share_rows = TPP * TILE // FEAT
-    order = [4, 5, 3, 2, 6, 7, 1]
-
-    def mail_copy(step):
-        to = (member + step) % FEAT
+    chip, chips = member // 2, FEAT // 2
+
+    def mail_place(step, other):
+        return (chip + step) % chips * 2 + core + other * (1 - 2 * core)
+
+    def mail_copy(step, other):
+        to = mail_place(step, other)
         return pltpu.make_async_remote_copy(
-            src_ref=mail.at[to], dst_ref=inbox.at[member], send_sem=mail_send.at[step - 1], recv_sem=mail_recv.at[step - 1],
-            device_id=(group, to), device_id_type=MESH)
-
-    for n in order:
-        to = (member + n) % FEAT
-        mail[to] = total[pl.ds(pl.multiple_of(to * share_rows, share_rows), share_rows), :].astype(jnp.bfloat16)
-        mail_copy(n).start()
-    inbox[member] = total[pl.ds(pl.multiple_of(member * share_rows, share_rows), share_rows), :].astype(jnp.bfloat16)
+            src_ref=mail.at[to], dst_ref=inbox.at[member], send_sem=mail_send.at[step * 2 + other],
+            recv_sem=mail_recv.at[step * 2 + other], device_id=(group, to), device_id_type=MESH)
+
+    mail_order = [(2, 0), (2, 1), (1, 0), (3, 0), (1, 1), (3, 1), (0, 1), (0, 0)]
+    columns = [panel_of[k] * NEED + HALF for k in range(N_FULL, len(ORDER))]
+    block = jnp.concatenate([parts[k, HALF:].reshape(HALF * TILE, TILE) for k in range(N_FULL, len(ORDER))], axis=0)
+    for step, other in mail_order:
+        to = mail_place(step, other)
+        for q in range(2):
+            row = jnp.concatenate([tile_mem[table[to * 2 + q, column + s]] for column in columns for s in range(HALF)], axis=1)
+            rows = pl.ds(pl.multiple_of((to * 2 + q) * TILE, TILE), TILE)
+            done = total[rows, :] + jnp.dot(row, block, preferred_element_type=jnp.float32)
+            place_rows = pl.ds(q * TILE, TILE)
+            if (step, other) == (0, 0):
+                inbox[to, place_rows, :] = done.astype(jnp.bfloat16)
+            else:
+                mail[to, place_rows, :] = done.astype(jnp.bfloat16)
+        if (step, other) != (0, 0):
+            mail_copy(step, other).start()
+
     weight_copy.wait()
-    for n in order:
-        mail_copy(n).wait_recv()
-    rows = jnp.concatenate([inbox[j] for j in range(FEAT)], axis=1)
     width = 256
-    for c in range(out.shape[1] // width):
-        cols = slice(c * width, (c + 1) * width)
-        mixed = jnp.dot(rows, weight_mem[:, cols], preferred_element_type=jnp.float32)
-        out[:, cols] = jnp.maximum(mixed, 0.0).astype(out.dtype)
+    arrivals = [0, 2, 3, 1]
+    for n, away in enumerate(arrivals):
+        back = (chips - away) % chips
+        for other in range(2):
+            if (back, other) != (0, 0):
+                mail_copy(back, other).wait_recv()
+        source = (chip + away) % chips
+        rows = jnp.concatenate([inbox[source * 2], inbox[source * 2 + 1]], axis=1)
+        depth = pl.ds(pl.multiple_of(source * 2 * TILE, 2 * TILE), 2 * TILE)
+        for c in range(out.shape[1] // width):
+            cols = slice(c * width, (c + 1) * width)
+            product = jnp.dot(rows, weight_mem[depth, cols], preferred_element_type=jnp.float32)
+            if n > 0:
+                product = product + mixed[:, cols]
+            if n < chips - 1:
+                mixed[:, cols] = product
+            else:
+                out[:, cols] = jnp.maximum(product, 0.0).astype(out.dtype)
     for w in INNER_LIST:
         for c in range(CHUNKS):
             inner_copy(w, c).wait_send()
     for w in LEAF_LIST:
-        leaf_copy(w).wait_send()
-    for n in order:
-        mail_copy(n).wait_send()
+        for part in range(2):
+            leaf_copy(w, part).wait_send()
+    for step, other in mail_order[:-1]:
+        mail_copy(step, other).wait_send()
 
 
 def per_device(features, tiles, tile_row, tile_panel, tile_slot, counts, need_list, weight):
@@ -230,20 +277,21 @@
             pltpu.SMEM((MAXT,), jnp.int32),
             pltpu.SMEM((MAXT,), jnp.int32),
             pltpu.SMEM((1,), jnp.int32),
-            pltpu.SMEM((5, GROUPS, NEED), jnp.int32),
+            pltpu.SMEM((5, NEED, GROUPS), jnp.int32),
             pltpu.SMEM((GROUPS,), jnp.int32),
             pltpu.VMEM((TPP * TILE, width), jnp.float32),
             pltpu.VMEM((FEAT * width, hidden), bf16),
             pltpu.VMEM((FEAT, share_rows, width), bf16),
             pltpu.VMEM((FEAT, share_rows, width), bf16),
+            pltpu.VMEM((share_rows, hidden), jnp.float32),
             dma((3,)), dma((TILE_DMAS,)), dma((9,)),
             dma((len(INNER) * CHUNKS,)), dma((len(INNER) * CHUNKS,)),
-            dma((len(LEAF),)), dma((len(LEAF),)),
-            dma((FEAT - 1,)), dma((FEAT - 1,)),
+            dma((2 * len(LEAF),)), dma((2 * len(LEAF),)),
+            dma((FEAT,)), dma((FEAT,)),
         ],
         compiler_params=pltpu.CompilerParams(collective_id=0, has_side_effects=True, vmem_limit_bytes=56 * 2**20),
         cost_estimate=pl.CostEstimate(flops=9 * 10**9, bytes_accessed=25 * 10**6, transcendentals=0),
-    )(features.reshape(TPP, TILE, width), tiles, tile_row, tile_panel, tile_slot, counts, need_list, weight)
+    )(features.reshape(TPP, TILE, width), tiles, tile_row, tile_panel, tile_slot, counts, need_list.transpose(0, 2, 1), weight)
 
 
 def solution(mesh):

time: 61.8 us -> 55.5 us (0.90)
  Pallas kernels: 57.5 us -> 52.8 us
  local copies, waits for them, and re-layouts: 3.46 us -> 1.87 us
    pallas_call x1, Pallas kernels: 57.5 us -> 52.8 us  [per_device(): pl.pallas_call(layer_kernel, out_shape=jax.ShapeDtypeStruct((share_rows,...]
    unnamed x2 -> x1, local copies, waits for them, and re-layouts: 3.46 us -> 1.87 us
where the time goes in v2:
time: 55.5 us; the launch traced here: 55.3 us
  Pallas kernels  52.8 us (95%)
  local copies, waits for them, and re-layouts  1.87 us (3%)
  between operations  0.66 us (1%)
    pallas_call x1, Pallas kernels, per_device(): pl.pallas_call(layer_kernel, out_shape=jax.ShapeDtypeStruct((share_rows,...  52.8 us
    unnamed x1, local copies, waits for them, and re-layouts  1.87 us

profile of v2, /device:TPU:1, one launch (start us, length us, event | category | flops | bytes accessed | tf_op | source)
XLA Modules:
  0.0 55.3 jit_solution(11705736959189458846)
XLA Ops:
  0.7 52.8 %shard_map.82 = bf16[256,1024]{1,0:T(8,128)(2,1)} custom-call(bf16[16,128,128]{2,1,0:T(8,128)(2,1)} %bitcast.2, bf16[640,128,128]{2,1,0:T(8,128)(2,1)} %tiles.1, s32[640]{0:T(1024)} %row_hbm.1, s32[640]{0:T(1024)} %panel_hbm.1, s32[640]{0:T(1024)} %slot_hbm.1, s32[1]{0:T(128)S(6)} %copy.10.count_hbm, s32[16,8,16]{2,1,0:T(8,128)} %bitcast.3, ...), custom_call_target="tpu_custom_call" | custom-call | flops 8999999488 | bytes 25000000 | tf_op jit(solution)/shard_map/pallas_call | solution.py:265
  53.5 1.9 %copy.11 = bf16[256,1024]{1,0:T(8,128)(2,1)} copy(bf16[256,1024]{1,0:T(8,128)(2,1)} %shard_map.82) | data formatting | bytes 1048576

commit v3 on v2

--- a/solution.py
+++ b/solution.py
@@ -67,6 +67,12 @@
         a, b = flip(first, v & 3), flip(second, v >> 2)
         return (a + core * (b - a)) * 4 + b + core * (a - b)
 
+    barrier = pltpu.get_barrier_semaphore()
+    for d in range(4):
+        pl.semaphore_signal(barrier, inc=1, device_id=(group_at(1 << d), member), device_id_type=MESH)
+    for step in range(1, FEAT):
+        pl.semaphore_signal(barrier, inc=1, device_id=(group, (member + step) % FEAT), device_id_type=MESH)
+
     own_copy = pltpu.make_async_copy(features, held0, local_sem.at[0])
     own_copy.start()
     small = [
@@ -81,12 +87,6 @@
     for copy in small:
         copy.start()
 
-    barrier = pltpu.get_barrier_semaphore()
-    for d in range(4):
-        pl.semaphore_signal(barrier, inc=1, device_id=(group_at(1 << d), member), device_id_type=MESH)
-    for step in range(1, FEAT):
-        pl.semaphore_signal(barrier, inc=1, device_id=(group, (member + step) % FEAT), device_id_type=MESH)
-
     share = MAXT // TILE_DMAS
     tile_copies = [
         pltpu.make_async_copy(tiles.at[pl.ds(i * share, share)], tile_mem.at[pl.ds(i * share, share)], tile_sem.at[i])
@@ -101,7 +101,7 @@
         i = INNER_LIST.index(w) * CHUNKS + c
         rows = pl.ds(c * PER, PER)
         return pltpu.make_async_remote_copy(
-            src_ref=held[v].at[rows], dst_ref=held[w].at[rows], send_sem=inner_send.at[i], recv_sem=inner_recv.at[i],
+            src_ref=(held[v] if v else features).at[rows], dst_ref=held[w].at[rows], send_sem=inner_send.at[i], recv_sem=inner_recv.at[i],
             device_id=(group_at(1 << d), member), device_id_type=MESH)
 
     def leaf_copy(w, part):
@@ -134,13 +134,13 @@
             for part in range(2):
                 leaf_copy(v, part).wait_recv()
 
-    own_copy.wait()
     pl.semaphore_wait(barrier, 4 + FEAT - 1)
     for c in range(CHUNKS):
         inner_copy(8, c).start()
         inner_copy(4, c).start()
     for copy in small:
         copy.wait()
+    own_copy.wait()
 
     for k, v in enumerate(ORDER):
         panel_of[k] = group_at(v)

time: 55.5 us -> 53.7 us (0.968)
  Pallas kernels: 52.8 us -> 50.9 us
    pallas_call x1, Pallas kernels: 52.8 us -> 50.9 us  [per_device(): pl.pallas_call(layer_kernel, out_shape=jax.ShapeDtypeStruct((share_rows,...]
where the time goes in v3:
time: 53.7 us; the launch traced here: 53.4 us
  Pallas kernels  50.9 us (95%)
  local copies, waits for them, and re-layouts  1.87 us (3%)
  between operations  0.66 us (1%)
    pallas_call x1, Pallas kernels, per_device(): pl.pallas_call(layer_kernel, out_shape=jax.ShapeDtypeStruct((share_rows,...  50.9 us
    unnamed x1, local copies, waits for them, and re-layouts  1.87 us

profile of v3, /device:TPU:1, one launch (start us, length us, event | category | flops | bytes accessed | tf_op | source)
XLA Modules:
  0.0 53.4 jit_solution(18276542177144899745)
XLA Ops:
  0.7 50.9 %shard_map.82 = bf16[256,1024]{1,0:T(8,128)(2,1)} custom-call(bf16[16,128,128]{2,1,0:T(8,128)(2,1)} %bitcast.2, bf16[640,128,128]{2,1,0:T(8,128)(2,1)} %tiles.1, s32[640]{0:T(1024)} %row_hbm.1, s32[640]{0:T(1024)} %panel_hbm.1, s32[640]{0:T(1024)} %slot_hbm.1, s32[1]{0:T(128)S(6)} %copy.10.count_hbm, s32[16,8,16]{2,1,0:T(8,128)} %bitcast.3, ...), custom_call_target="tpu_custom_call" | custom-call | flops 8999999488 | bytes 25000000 | tf_op jit(solution)/shard_map/pallas_call | solution.py:265
  51.6 1.9 %copy.11 = bf16[256,1024]{1,0:T(8,128)(2,1)} copy(bf16[256,1024]{1,0:T(8,128)(2,1)} %shard_map.82) | data formatting | bytes 1048576

commit v4 on v3

--- a/solution.py
+++ b/solution.py
@@ -37,11 +37,11 @@
     0: [("use", 0)],
     1: [("use", 8), ("in", 9, 1)],
     2: [("in", 4, 3), ("in", 9, 2), ("use", 4), ("send", 1), ("send", 12)],
-    3: [("in", 9, 3), ("use", 9)],
-    4: [("in", 6, 0), ("in", 6, 1), ("in", 6, 2), ("in", 6, 3), ("use", 6), ("send", 2), ("send", 14), ("send", 5), ("send", 13)],
+    3: [("in", 9, 3), ("use", 9), ("send", 5), ("send", 13)],
+    4: [("in", 6, 0), ("in", 6, 1), ("in", 6, 2), ("in", 6, 3), ("use", 6), ("send", 2), ("send", 14), ("send", 7)],
     5: [("get", 1)],
     6: [("get", 12)],
-    7: [("in", 11, 0), ("in", 11, 1), ("in", 11, 2), ("in", 11, 3), ("use", 11), ("send", 7), ("send", 15), ("send", 3), ("send", 10)],
+    7: [("in", 11, 0), ("in", 11, 1), ("in", 11, 2), ("in", 11, 3), ("use", 11), ("send", 15), ("send", 3), ("send", 10)],
     8: [("get", 2)],
     9: [("get", 14)],
     10: [("get", 5)],
@@ -159,10 +159,12 @@
     total[...] = jnp.zeros_like(total)
     table_copy.wait()
 
-    for event in BEFORE:
+    for event in BEFORE[:4]:
         perform(event)
     for copy in tile_copies:
         copy.wait()
+    for event in BEFORE[4:]:
+        perform(event)
 
     def step(k, carry):
         for at, events in STEPS.items():

time: 53.7 us -> 53.7 us (level)
  no operation moved by 1% of the time
where the time goes in v4:
time: 53.7 us; the launch traced here: 53.4 us
  Pallas kernels  50.9 us (95%)
  local copies, waits for them, and re-layouts  1.87 us (3%)
  between operations  0.66 us (1%)
    pallas_call x1, Pallas kernels, per_device(): pl.pallas_call(layer_kernel, out_shape=jax.ShapeDtypeStruct((share_rows,...  50.9 us
    unnamed x1, local copies, waits for them, and re-layouts  1.87 us

profile of v4, /device:TPU:1, one launch (start us, length us, event | category | flops | bytes accessed | tf_op | source)
XLA Modules:
  0.0 53.4 jit_solution(5603601676919872506)
XLA Ops:
  0.7 50.9 %shard_map.82 = bf16[256,1024]{1,0:T(8,128)(2,1)} custom-call(bf16[16,128,128]{2,1,0:T(8,128)(2,1)} %bitcast.2, bf16[640,128,128]{2,1,0:T(8,128)(2,1)} %tiles.1, s32[640]{0:T(1024)} %row_hbm.1, s32[640]{0:T(1024)} %panel_hbm.1, s32[640]{0:T(1024)} %slot_hbm.1, s32[1]{0:T(128)S(6)} %copy.10.count_hbm, s32[16,8,16]{2,1,0:T(8,128)} %bitcast.3, ...), custom_call_target="tpu_custom_call" | custom-call | flops 8999999488 | bytes 25000000 | tf_op jit(solution)/shard_map/pallas_call | solution.py:267
  51.6 1.9 %copy.11 = bf16[256,1024]{1,0:T(8,128)(2,1)} copy(bf16[256,1024]{1,0:T(8,128)(2,1)} %shard_map.82) | data formatting | bytes 1048576
